TPU v7x, 768 devices: a whole 4x8x12 slice. The times are simulated.
768 devices in a mesh: comp: 32 (over x, y), tile: 24 (over z, core).
Axes of the slice: x: 4, y: 8, z: 12, core: 2. Of those that a mesh axis runs over, the one named last changes fastest.
Arguments:
- atm_state: float32 [128, 512, 3072], P(None, 'comp', 'tile'), may hold values from -6 to 6
- ocean_state: float32 [48, 512, 3072], P(None, 'comp', 'tile'), may hold values from -6 to 6
- atm_rate: float32 [128], replicated, may hold values from 0.02 to 0.24
- ocean_rate: float32 [48], replicated, may hold values from 0.02 to 0.24
- ocean_mask: int32 [512, 24], P('comp', 'tile'), may hold values 0 or 1
- remap_weight: bfloat16 [32, 1152, 128, 128], P('comp', 'tile'), may hold values from -0.5 to 0.5
- pair_src: int32 [32, 1152], P('comp', 'tile'), may hold values from 0 to 383, as said below
- pair_tgt: int32 [32, 1152], P('comp', 'tile'), may hold values from 0 to 383, as said below
- pair_count: int32 [32, 24], P('comp', 'tile'), may hold values from 24 to 48, as said below
Outputs:
- atm_next: float32 [128, 512, 3072], P(None, 'comp', 'tile')
- ocean_next: float32 [48, 512, 3072], P(None, 'comp', 'tile')
Inputs may be any that keep to these rules, and one draw needn't show every extreme that they name: `pair_src`: entry d * 48 + j of row b names atmosphere tile e * 16 + y of band b. Among the first pair_count[b, d] entries of device d at most 3 have the same e, and every device has 3 live entries with one same e. `pair_tgt`: entry d * 48 + j of row b names ocean tile e * 16 + y of band b. Among the first pair_count[b, d] entries of device d at most 3 have the same e, and every device has 3 live entries with one same e. `pair_count`: each row b has some device with 48 live slots.
All inputs are finite; a program needn't handle non-finite values. No bound on the sum of `ocean_mask` on one device may be relied on, other than what follows from the above.
Results may differ from a plain program's by a relative error of at most 0.002.
Values may be sent and summed in bfloat16 or wider, within the bound.
A program may use at most 32 MiB of HBM per device.

v0:
```python
import jax
import jax.numpy as jnp
from jax import lax
from jax.sharding import PartitionSpec as P

SURF = 8


def padded_2(block, sides, width):
    for axis, dim in sides:
        count = lax.axis_size(axis)
        forward = [(i, i + 1) for i in range(count - 1)]
        forward.append((count - 1, 0))
        backward = [(target, source) for source, target in forward]
        low = lax.ppermute(
            lax.slice_in_dim(block, block.shape[dim] - width, None, axis=dim), axis, forward
        )
        high = lax.ppermute(lax.slice_in_dim(block, 0, width, axis=dim), axis, backward)
        block = jnp.concatenate([low, block, high], axis=dim)
    return block


def relax(padded, spread):
    center = padded[:, 1:-1, 1:-1]
    beside_all = (
        padded[:, 2:, 1:-1] + padded[:, :-2, 1:-1] + padded[:, 1:-1, 2:] + padded[:, 1:-1, :-2]
    )
    return center + spread[:, None, None] * (beside_all - 4.0 * center)


def ghosts(padded, width):
    row_total = padded.shape[1]
    row_index = jnp.arange(row_total)
    position = lax.axis_index("comp")
    at_first = jnp.logical_and(row_index < width, position == 0)
    at_last = jnp.logical_and(row_index >= row_total - width, position == lax.axis_size("comp") - 1)
    retain = jnp.logical_not(jnp.logical_or(at_first, at_last)).astype(jnp.float32)
    return padded * retain[None, :, None]


def shards(
    atm_state,
    ocean_state,
    atm_rate,
    ocean_rate,
    ocean_mask,
    remap_weight,
    pair_src,
    pair_tgt,
    pair_count,
):
    atm_rows = atm_state.shape[1]
    ocean_rows = ocean_state.shape[1]
    cell_total = atm_state.shape[2]
    pair_total = pair_src.shape[1]
    wet_rows = ocean_mask[:, 0].astype(jnp.float32)
    atm_source = atm_state[:SURF].astype(jnp.bfloat16)
    ocean_source = (ocean_state[:SURF] * wet_rows[None, :, None]).astype(jnp.bfloat16)
    atm_band, ocean_band = (
        lax.all_gather(atm_source, "tile", axis=1, tiled=True),
        lax.all_gather(ocean_source, "tile", axis=1, tiled=True),
    )
    anchor = pair_src[0]
    target = pair_tgt[0]
    active = jnp.arange(pair_total) < pair_count[0, 0]
    active_float = active.astype(jnp.float32)[:, None, None]
    weights = remap_weight[0]
    forward = (
        jnp.einsum(
            "fpt,pts->pfs",
            jnp.take(atm_band, anchor, axis=1),
            weights,
            preferred_element_type=jnp.float32,
        )
        * active_float
    )
    reverse = (
        jnp.einsum(
            "fps,pts->pft",
            jnp.take(ocean_band, target, axis=1),
            weights,
            preferred_element_type=jnp.float32,
        )
        * active_float
    )
    band_rows = atm_rows + ocean_rows
    ahead_codes = jnp.where(
        active, target // ocean_rows * band_rows + atm_rows + target % ocean_rows, -1
    )
    back_codes = jnp.where(active, anchor // atm_rows * band_rows + anchor % atm_rows, -1)
    ahead_flat = forward.reshape(pair_total, -1)
    back_flat = reverse.reshape(pair_total, -1)
    row_codes = jnp.arange(band_rows * lax.axis_size("tile"))
    ahead_hot = (row_codes[:, None] == ahead_codes[None, :]).astype(jnp.float32)
    back_hot = (row_codes[:, None] == back_codes[None, :]).astype(jnp.float32)
    summed = lax.psum_scatter(
        jnp.dot(
            ahead_hot,
            ahead_flat,
            precision=lax.Precision.HIGHEST,
            preferred_element_type=jnp.float32,
        )
        + jnp.dot(
            back_hot, back_flat, precision=lax.Precision.HIGHEST, preferred_element_type=jnp.float32
        ),
        "tile",
        scatter_dimension=0,
        tiled=True,
    )
    atm_force = summed[:atm_rows].reshape(atm_rows, SURF, cell_total)
    ocean_force = summed[atm_rows:].reshape(ocean_rows, SURF, cell_total)
    atm_stepped = atm_state
    ocean_stepped = ocean_state
    for repeat in range(2):
        atm_stepped = relax(
            ghosts(padded_2(atm_stepped, (("comp", 1), ("tile", 2)), 1), 1), atm_rate
        )
        ocean_stepped = relax(
            ghosts(padded_2(ocean_stepped, (("comp", 1), ("tile", 2)), 1), 1), ocean_rate
        )
    atm_next = atm_stepped.at[:SURF].add(jnp.transpose(atm_force, (1, 0, 2)))
    ocean_next = ocean_stepped.at[:SURF].add(
        jnp.transpose(ocean_force, (1, 0, 2)) * wet_rows[None, :, None]
    )
    return (atm_next, ocean_next)


def solution(mesh):
    return jax.shard_map(
        shards,
        mesh=mesh,
        in_specs=(
            P(None, "comp", "tile"),
            P(None, "comp", "tile"),
            P(),
            P(),
            P("comp", "tile"),
            P("comp", "tile", None, None),
            P("comp", "tile"),
            P("comp", "tile"),
            P("comp", "tile"),
        ),
        out_specs=(P(None, "comp", "tile"), P(None, "comp", "tile")),
        check_vma=False,
    )
```

profile of v0, /device:TPU:1, one launch (start us, length us, event | category | flops | bytes accessed | tf_op | source)
XLA Modules:
  0.0 189.5 jit_solution(9809638579662079551)
XLA Ops:
  13.2 36.6 %all_gather.6 = bf16[8,384,128]{2,0,1:T(8,128)(2,1)S(1)} all-gather(bf16[8,16,128]{2,0,1:T(8,128)(2,1)S(1)} %copy.130), channel_id=1, replica_groups=mesh['comp'=32,'tile'=24] {'tile'}, dimensions={1}, use_global_device_ids=true | all-gather | bytes 819200 | tf_op jit(solution)/shard_map/all_gather | solution.py:60
  50.9 22.9 %all_gather.7 = bf16[8,384,128]{2,0,1:T(8,128)(2,1)S(1)} all-gather(bf16[8,16,128]{2,0,1:T(8,128)(2,1)S(1)} %fusion.36), channel_id=1, replica_groups=mesh['comp'=32,'tile'=24] {'tile'}, dimensions={1}, use_global_device_ids=true | all-gather | bytes 819200 | tf_op jit(solution)/shard_map/all_gather | solution.py:61
  77.0 3.0 %fusion.22 = f32[768,1024]{1,0:T(8,128)} fusion(f32[6,8,8,128]{3,2,1,0:T(8,128)S(1)} %bitcast.53, s32[48]{0:T(128)S(1)} %copy-done.11), kind=kOutput, calls=%fused_computation.41 | convolution fusion | flops 453021696 | bytes 3342528 | tf_op jit(solution)/shard_map/dot_general | solution.py:97
  81.6 4.9 %convolution_add_fusion = f32[768,1024]{1,0:T(8,128)} fusion(f32[768,1024]{1,0:T(8,128)} %fusion.22, f32[6,8,8,128]{3,2,1,0:T(8,128)S(1)} %bitcast.52, s32[48]{0:T(128)S(1)} %copy-done.10), kind=kOutput, calls=%fused_computation.2 | convolution fusion | flops 453808128 | bytes 6488256 | tf_op jit(solution)/shard_map/dot_general | solution.py:103
  86.6 3.3 %collective-permute-start.8 = (f32[48,1,128]{2,0,1:T(8,128)S(1)}, f32[48,1,128]{2,0,1:T(8,128)S(1)}, u32[]{:S(2)}, u32[]{:S(2)}) collective-permute-start(f32[48,1,128]{2,0,1:T(8,128)S(1)} %get-tuple-element.52), channel_id=1, source_target_pairs={{0,24},{24,48},{48,72},{72,96},{96,120},{120,144},{144,168},{168,1... | collective-permute-start | bytes 73736 | tf_op jit(solution)/shard_map/ppermute | solution.py:15
  89.9 6.0 %collective-permute-start.9 = (f32[48,1,128]{2,0,1:T(8,128)S(1)}, f32[48,1,128]{2,0,1:T(8,128)S(1)}, u32[]{:S(2)}, u32[]{:S(2)}) collective-permute-start(f32[48,1,128]{2,0,1:T(8,128)S(1)} %get-tuple-element.51), channel_id=1, source_target_pairs={{24,0},{48,24},{72,48},{96,72},{120,96},{144,120},{168,144},{192,1... | collective-permute-start | bytes 73736 | tf_op jit(solution)/shard_map/ppermute | solution.py:18
  97.3 2.3 %collective-permute-start.10 = (f32[48,18,1]{0,1,2:T(8,128)S(1)}, f32[48,18,1]{0,1,2:T(8,128)S(1)}, u32[]{:S(2)}, u32[]{:S(2)}) collective-permute-start(f32[48,18,1]{0,1,2:T(8,128)S(1)} %copy.105), channel_id=1, source_target_pairs={{0,1},{1,2},{2,3},{3,4},{4,5},{5,6},{6,7},{7,8},{8,9},{9,10},{10,1... | collective-permute-start | bytes 10376 | tf_op jit(solution)/shard_map/ppermute | solution.py:15
  99.9 1.9 copy.96
  104.0 1.6 maximum_multiply_fusion.2
  106.1 1.9 %collective-permute-start.12 = (f32[48,1,128]{2,0,1:T(8,128)S(1)}, f32[48,1,128]{2,0,1:T(8,128)S(1)}, u32[]{:S(2)}, u32[]{:S(2)}) collective-permute-start(f32[48,1,128]{2,0,1:T(8,128)S(1)} %get-tuple-element.49), channel_id=1, source_target_pairs={{0,24},{24,48},{48,72},{72,96},{96,120},{120,144},{144,168},{168,1... | collective-permute-start | bytes 73736 | tf_op jit(solution)/shard_map/ppermute | solution.py:15
  108.0 7.8 %collective-permute-start.13 = (f32[48,1,128]{2,0,1:T(8,128)S(1)}, f32[48,1,128]{2,0,1:T(8,128)S(1)}, u32[]{:S(2)}, u32[]{:S(2)}) collective-permute-start(f32[48,1,128]{2,0,1:T(8,128)S(1)} %get-tuple-element.50), channel_id=1, source_target_pairs={{24,0},{48,24},{72,48},{96,72},{120,96},{144,120},{168,144},{192,1... | collective-permute-start | bytes 73736 | tf_op jit(solution)/shard_map/ppermute | solution.py:18
  115.9 1.9 %collective-permute-start = (f32[128,1,128]{0,1,2:T(1,128)S(1)}, f32[128,1,128]{0,1,2:T(1,128)S(1)}, u32[]{:S(2)}, u32[]{:S(2)}) collective-permute-start(f32[128,1,128]{0,1,2:T(1,128)S(1)} %get-tuple-element.43), channel_id=1, source_target_pairs={{0,24},{24,48},{48,72},{72,96},{96,120},{120,144},{144,168},{168,1... | collective-permute-start | bytes 196616 | tf_op jit(solution)/shard_map/ppermute | solution.py:15
  117.8 6.7 %collective-permute-start.1 = (f32[128,1,128]{0,1,2:T(1,128)S(1)}, f32[128,1,128]{0,1,2:T(1,128)S(1)}, u32[]{:S(2)}, u32[]{:S(2)}) collective-permute-start(f32[128,1,128]{0,1,2:T(1,128)S(1)} %get-tuple-element.44), channel_id=1, source_target_pairs={{24,0},{48,24},{72,48},{96,72},{120,96},{144,120},{168,144},{192,1... | collective-permute-start | bytes 196616 | tf_op jit(solution)/shard_map/ppermute | solution.py:18
  126.4 2.4 %collective-permute-start.2 = (f32[128,18,1]{0,1,2:T(8,128)}, f32[128,18,1]{0,1,2:T(8,128)}, u32[]{:S(2)}, u32[]{:S(2)}) collective-permute-start(f32[128,18,1]{0,1,2:T(8,128)} %get-tuple-element.39), channel_id=1, source_target_pairs={{0,1},{1,2},{2,3},{3,4},{4,5},{5,6},{6,7},{7,8},{8,9},{9,10},{10,1... | collective-permute-start | bytes 27656 | tf_op jit(solution)/shard_map/ppermute | solution.py:15
  129.8 1.9 copy.109
  131.7 1.7 collective-permute-start.14
  137.7 1.7 copy.112
  141.7 1.9 %collective-permute-start.4 = (f32[128,1,128]{0,1,2:T(1,128)S(1)}, f32[128,1,128]{0,1,2:T(1,128)S(1)}, u32[]{:S(2)}, u32[]{:S(2)}) collective-permute-start(f32[128,1,128]{0,1,2:T(1,128)S(1)} %get-tuple-element.41), channel_id=1, source_target_pairs={{0,24},{24,48},{48,72},{72,96},{96,120},{120,144},{144,168},{168,1... | collective-permute-start | bytes 196616 | tf_op jit(solution)/shard_map/ppermute | solution.py:15
  143.6 7.5 %collective-permute-start.5 = (f32[128,1,128]{0,1,2:T(1,128)S(1)}, f32[128,1,128]{0,1,2:T(1,128)S(1)}, u32[]{:S(2)}, u32[]{:S(2)}) collective-permute-start(f32[128,1,128]{0,1,2:T(1,128)S(1)} %get-tuple-element.42), channel_id=1, source_target_pairs={{24,0},{48,24},{72,48},{96,72},{120,96},{144,120},{168,144},{192,1... | collective-permute-start | bytes 196616 | tf_op jit(solution)/shard_map/ppermute | solution.py:18
  153.2 2.4 %collective-permute-start.7 = (f32[128,18,1]{0,1,2:T(8,128)S(1)}, f32[128,18,1]{0,1,2:T(8,128)S(1)}, u32[]{:S(2)}, u32[]{:S(2)}) collective-permute-start(f32[128,18,1]{0,1,2:T(8,128)S(1)} %get-tuple-element.38), channel_id=1, source_target_pairs={{1,0},{2,1},{3,2},{4,3},{5,4},{6,5},{7,6},{8,7},{9,8},{10,9},{11,1... | collective-permute-start | bytes 27656 | tf_op jit(solution)/shard_map/ppermute | solution.py:18
  157.1 12.6 %reduce-scatter.2.cloned.1.call-done = f32[32,1024]{1,0:T(8,128)} async-done(((f32[768,1024]{1,0:T(8,128)}), f32[32,1024]{1,0:T(8,128)}) %reduce-scatter.2.cloned.1.call-update) | async-done | bytes 131088 | tf_op jit(solution)/shard_map/reduce_scatter | solution.py:96
  173.0 2.3 %slice_add_fusion = f32[8,16,128]{0,1,2:T(8,128)} fusion(f32[128,16,128]{0,1,2:T(8,128)S(1)} %fusion.12, f32[16,8,128]{1,0,2:T(8,128)} %copy.101), kind=kLoop, calls=%fused_computation.11 | loop fusion | flops 16384 | bytes 196608 | tf_op jit(solution)/shard_map/add | solution.py:121
  175.3 5.7 %scatter-add.6 = f32[128,16,128]{0,1,2:T(8,128)S(1)} dynamic-update-slice(f32[128,16,128]{0,1,2:T(8,128)S(1)} %fusion.12, f32[8,16,128]{0,1,2:T(8,128)} %slice_add_fusion, s32[]{:T(128)} %constant.108.clone.1, s32[]{:T(128)} %constant.108.clone.1, s32[]{:T(128)} %constant.108.clone.1) | dynamic-update-slice | bytes 131076 | tf_op jit(solution)/shard_map/scatter-add | solution.py:121
  181.0 1.6 copy.113
  (102 shorter events, 31.8 us)
Async XLA Ops:
  7.2 68.4 %copy-start = (bf16[1,48,128,128]{3,2,1,0:T(8,128)(2,1)S(1)}, bf16[1,48,128,128]{3,2,1,0:T(8,128)(2,1)}, u32[]{:S(2)}) copy-start(bf16[1,48,128,128]{3,2,1,0:T(8,128)(2,1)} %param.20) | copy-start | bytes 4718596
  7.2 42.6 %copy-start.12 = (s32[1,48]{1,0:T(1,128)S(1)}, s32[1,48]{1,0:T(1,128)}, u32[]{:S(2)}) copy-start(s32[1,48]{1,0:T(1,128)} %param.22) | copy-start | bytes 580
  7.2 43.2 %copy-start.13 = (s32[16,1]{0,1:T(1,128)S(1)}, s32[16,1]{0,1:T(1,128)}, u32[]{:S(2)}) copy-start(s32[16,1]{0,1:T(1,128)} %param.19) | copy-start | bytes 196
  7.2 162.5 %reduce-scatter.2.cloned.1.call-start = ((), (), s32[]{:S(2)}) async-start(), calls=%async_computation.1 | async-start | bytes 3276800 | tf_op jit(solution)/shard_map/reduce_scatter | solution.py:96
  7.2 66.5 %copy-start.14 = (s32[1,48]{1,0:T(1,128)S(1)}, s32[1,48]{1,0:T(1,128)}, u32[]{:S(2)}) copy-start(s32[1,48]{1,0:T(1,128)} %param.21) | copy-start | bytes 580
  86.6 9.4 %collective-permute-start.8 = (f32[48,1,128]{2,0,1:T(8,128)S(1)}, f32[48,1,128]{2,0,1:T(8,128)S(1)}, u32[]{:S(2)}, u32[]{:S(2)}) collective-permute-start(f32[48,1,128]{2,0,1:T(8,128)S(1)} %get-tuple-element.52), channel_id=1, source_target_pairs={{0,24},{24,48},{48,72},{72,96},{96,120},{120,144},{144,168},{168,1... | collective-permute-start | bytes 73736 | tf_op jit(solution)/shard_map/ppermute | solution.py:15
  89.9 6.9 %collective-permute-start.9 = (f32[48,1,128]{2,0,1:T(8,128)S(1)}, f32[48,1,128]{2,0,1:T(8,128)S(1)}, u32[]{:S(2)}, u32[]{:S(2)}) collective-permute-start(f32[48,1,128]{2,0,1:T(8,128)S(1)} %get-tuple-element.51), channel_id=1, source_target_pairs={{24,0},{48,24},{72,48},{96,72},{120,96},{144,120},{168,144},{192,1... | collective-permute-start | bytes 73736 | tf_op jit(solution)/shard_map/ppermute | solution.py:18
  97.3 4.5 %collective-permute-start.10 = (f32[48,18,1]{0,1,2:T(8,128)S(1)}, f32[48,18,1]{0,1,2:T(8,128)S(1)}, u32[]{:S(2)}, u32[]{:S(2)}) collective-permute-start(f32[48,18,1]{0,1,2:T(8,128)S(1)} %copy.105), channel_id=1, source_target_pairs={{0,1},{1,2},{2,3},{3,4},{4,5},{5,6},{6,7},{7,8},{8,9},{9,10},{10,1... | collective-permute-start | bytes 10376 | tf_op jit(solution)/shard_map/ppermute | solution.py:15
  99.8 3.1 %collective-permute-start.11 = (f32[48,18,1]{0,1,2:T(8,128)S(1)}, f32[48,18,1]{0,1,2:T(8,128)S(1)}, u32[]{:S(2)}, u32[]{:S(2)}) collective-permute-start(f32[48,18,1]{0,1,2:T(8,128)S(1)} %copy.106), channel_id=1, source_target_pairs={{1,0},{2,1},{3,2},{4,3},{5,4},{6,5},{7,6},{8,7},{9,8},{10,9},{11,1... | collective-permute-start | bytes 10376 | tf_op jit(solution)/shard_map/ppermute | solution.py:18
  106.1 18.4 %collective-permute-start.12 = (f32[48,1,128]{2,0,1:T(8,128)S(1)}, f32[48,1,128]{2,0,1:T(8,128)S(1)}, u32[]{:S(2)}, u32[]{:S(2)}) collective-permute-start(f32[48,1,128]{2,0,1:T(8,128)S(1)} %get-tuple-element.49), channel_id=1, source_target_pairs={{0,24},{24,48},{48,72},{72,96},{96,120},{120,144},{144,168},{168,1... | collective-permute-start | bytes 73736 | tf_op jit(solution)/shard_map/ppermute | solution.py:15
  108.0 16.5 %collective-permute-start.13 = (f32[48,1,128]{2,0,1:T(8,128)S(1)}, f32[48,1,128]{2,0,1:T(8,128)S(1)}, u32[]{:S(2)}, u32[]{:S(2)}) collective-permute-start(f32[48,1,128]{2,0,1:T(8,128)S(1)} %get-tuple-element.50), channel_id=1, source_target_pairs={{24,0},{48,24},{72,48},{96,72},{120,96},{144,120},{168,144},{192,1... | collective-permute-start | bytes 73736 | tf_op jit(solution)/shard_map/ppermute | solution.py:18
  115.9 8.7 %collective-permute-start = (f32[128,1,128]{0,1,2:T(1,128)S(1)}, f32[128,1,128]{0,1,2:T(1,128)S(1)}, u32[]{:S(2)}, u32[]{:S(2)}) collective-permute-start(f32[128,1,128]{0,1,2:T(1,128)S(1)} %get-tuple-element.43), channel_id=1, source_target_pairs={{0,24},{24,48},{48,72},{72,96},{96,120},{120,144},{144,168},{168,1... | collective-permute-start | bytes 196616 | tf_op jit(solution)/shard_map/ppermute | solution.py:15
  117.8 8.0 %collective-permute-start.1 = (f32[128,1,128]{0,1,2:T(1,128)S(1)}, f32[128,1,128]{0,1,2:T(1,128)S(1)}, u32[]{:S(2)}, u32[]{:S(2)}) collective-permute-start(f32[128,1,128]{0,1,2:T(1,128)S(1)} %get-tuple-element.44), channel_id=1, source_target_pairs={{24,0},{48,24},{72,48},{96,72},{120,96},{144,120},{168,144},{192,1... | collective-permute-start | bytes 196616 | tf_op jit(solution)/shard_map/ppermute | solution.py:18
  126.4 12.9 %collective-permute-start.2 = (f32[128,18,1]{0,1,2:T(8,128)}, f32[128,18,1]{0,1,2:T(8,128)}, u32[]{:S(2)}, u32[]{:S(2)}) collective-permute-start(f32[128,18,1]{0,1,2:T(8,128)} %get-tuple-element.39), channel_id=1, source_target_pairs={{0,1},{1,2},{2,3},{3,4},{4,5},{5,6},{6,7},{7,8},{8,9},{9,10},{10,1... | collective-permute-start | bytes 27656 | tf_op jit(solution)/shard_map/ppermute | solution.py:15
  128.8 10.5 %collective-permute-start.3 = (f32[128,18,1]{0,1,2:T(8,128)}, f32[128,18,1]{0,1,2:T(8,128)}, u32[]{:S(2)}, u32[]{:S(2)}) collective-permute-start(f32[128,18,1]{0,1,2:T(8,128)} %get-tuple-element.40), channel_id=1, source_target_pairs={{1,0},{2,1},{3,2},{4,3},{5,4},{6,5},{7,6},{8,7},{9,8},{10,9},{11,1... | collective-permute-start | bytes 27656 | tf_op jit(solution)/shard_map/ppermute | solution.py:18
  131.7 3.9 %collective-permute-start.14 = (f32[48,18,1]{0,1,2:T(8,128)}, f32[48,18,1]{0,1,2:T(8,128)}, u32[]{:S(2)}, u32[]{:S(2)}) collective-permute-start(f32[48,18,1]{0,1,2:T(8,128)} %copy.109), channel_id=1, source_target_pairs={{0,1},{1,2},{2,3},{3,4},{4,5},{5,6},{6,7},{7,8},{8,9},{9,10},{10,1... | collective-permute-start | bytes 10376 | tf_op jit(solution)/shard_map/ppermute | solution.py:15
  134.2 3.4 %collective-permute-start.15 = (f32[48,18,1]{0,1,2:T(8,128)}, f32[48,18,1]{0,1,2:T(8,128)}, u32[]{:S(2)}, u32[]{:S(2)}) collective-permute-start(f32[48,18,1]{0,1,2:T(8,128)} %copy.110), channel_id=1, source_target_pairs={{1,0},{2,1},{3,2},{4,3},{5,4},{6,5},{7,6},{8,7},{9,8},{10,9},{11,1... | collective-permute-start | bytes 10376 | tf_op jit(solution)/shard_map/ppermute | solution.py:18
  140.5 10.6 %copy-start.1 = (f32[48,18,1]{2,0,1:T(8,128)S(1)}, f32[48,18,1]{2,0,1:T(8,128)}, u32[]{:S(2)}) copy-start(f32[48,18,1]{2,0,1:T(8,128)} %copy.112) | copy-start | bytes 10372
  140.5 10.6 %copy-start.5 = (f32[48,1,128]{2,0,1:T(8,128)S(1)}, f32[48,1,128]{2,0,1:T(8,128)}, u32[]{:S(2)}) copy-start(f32[48,1,128]{2,0,1:T(8,128)} %copy-done.4) | copy-start | bytes 73732
  141.7 9.9 %collective-permute-start.4 = (f32[128,1,128]{0,1,2:T(1,128)S(1)}, f32[128,1,128]{0,1,2:T(1,128)S(1)}, u32[]{:S(2)}, u32[]{:S(2)}) collective-permute-start(f32[128,1,128]{0,1,2:T(1,128)S(1)} %get-tuple-element.41), channel_id=1, source_target_pairs={{0,24},{24,48},{48,72},{72,96},{96,120},{120,144},{144,168},{168,1... | collective-permute-start | bytes 196616 | tf_op jit(solution)/shard_map/ppermute | solution.py:15
  143.6 8.6 %collective-permute-start.5 = (f32[128,1,128]{0,1,2:T(1,128)S(1)}, f32[128,1,128]{0,1,2:T(1,128)S(1)}, u32[]{:S(2)}, u32[]{:S(2)}) collective-permute-start(f32[128,1,128]{0,1,2:T(1,128)S(1)} %get-tuple-element.42), channel_id=1, source_target_pairs={{24,0},{48,24},{72,48},{96,72},{120,96},{144,120},{168,144},{192,1... | collective-permute-start | bytes 196616 | tf_op jit(solution)/shard_map/ppermute | solution.py:18
  152.3 4.0 %collective-permute-start.6 = (f32[128,18,1]{0,1,2:T(8,128)S(1)}, f32[128,18,1]{0,1,2:T(8,128)S(1)}, u32[]{:S(2)}, u32[]{:S(2)}) collective-permute-start(f32[128,18,1]{0,1,2:T(8,128)S(1)} %get-tuple-element.37), channel_id=1, source_target_pairs={{0,1},{1,2},{2,3},{3,4},{4,5},{5,6},{6,7},{7,8},{8,9},{9,10},{10,1... | collective-permute-start | bytes 27656 | tf_op jit(solution)/shard_map/ppermute | solution.py:15
  153.2 3.2 %collective-permute-start.7 = (f32[128,18,1]{0,1,2:T(8,128)S(1)}, f32[128,18,1]{0,1,2:T(8,128)S(1)}, u32[]{:S(2)}, u32[]{:S(2)}) collective-permute-start(f32[128,18,1]{0,1,2:T(8,128)S(1)} %get-tuple-element.38), channel_id=1, source_target_pairs={{1,0},{2,1},{3,2},{4,3},{5,4},{6,5},{7,6},{8,7},{9,8},{10,9},{11,1... | collective-permute-start | bytes 27656 | tf_op jit(solution)/shard_map/ppermute | solution.py:18
  156.7 13.9 %copy-start.9 = (f32[16]{0:T(128)S(1)}, f32[16]{0:T(128)}, u32[]{:S(2)}) copy-start(f32[16]{0:T(128)} %copy-done.8) | copy-start | bytes 196
  (8 other events, 24.8 us)
Sparse Core Ops, SparseCore 0:
  86.7 82.9 reduce-scatter.1
where the time goes:
time: 193 us; the launch traced here: 189 us
  blocking collectives  59.5 us (31%)
  starting transfers between devices  48 us (25%)
  local copies, waits for them, and re-layouts  25.9 us (13%)
  waiting for transfers between devices  17.2 us (9%)
  between operations  15.1 us (8%)
  other arithmetic  13.4 us (7%)
  matrix products  10.4 us (5%)
    all_gather x1, blocking collectives, shards(): lax.all_gather(atm_source, 'tile', axis=1, tiled=True)  36.6 us
    ppermute x8, starting transfers between devices, padded_2(): lax.ppermute(lax.slice_in_dim(block, 0, width, axis=dim), axis, backward)  31.4 us
    all_gather x1, blocking collectives, shards(): lax.all_gather(ocean_source, 'tile', axis=1, tiled=True)  22.9 us
    ppermute x8, starting transfers between devices, padded_2(): lax.ppermute(lax.slice_in_dim(block, block.shape[dim] - width, None, axis...  16.5 us
    reduce_scatter x1, waiting for transfers between devices, shards(): lax.psum_scatter(jnp.dot(ahead_hot, ahead_flat, precision=lax.Precision.H...  12.6 us
    unnamed x40, local copies, waits for them, and re-layouts  6.98 us
    scatter-add x1, local copies, waits for them, and re-layouts, shards(): atm_next = atm_stepped.at[:SURF].add(jnp.transpose(atm_force, (1, 0, 2)))  5.74 us
    dot_general x1, matrix products, shards(): jnp.dot(back_hot, back_flat, precision=lax.Precision.HIGHEST, preferred_e...  4.93 us
  transfers between devices with their start and end apart: 17, of which 9 were waited for; matrix products, arithmetic and copies ran while one was open for 9% of the time, Pallas kernels for 0%

commit v1 on v0

v1 whole, which is shorter than its diff:
```python
import functools

import jax
import jax.numpy as jnp
from jax import lax
from jax.experimental import pallas as pl
from jax.experimental.pallas import tpu as pltpu
from jax.sharding import PartitionSpec as P

SURF = 8
LANES = 128
ROWS = 16
CAP = 3
EMPTY = 100.0
F32 = jnp.float32
BF16 = jnp.bfloat16
MESH = pl.DeviceIdType.MESH


def lanes_of(shape):
    return lax.broadcasted_iota(jnp.int32, shape, 1)


def rows_of(shape):
    return lax.broadcasted_iota(jnp.int32, shape, 0)


def as_column(row, size):
    shape = (size, size)
    spread = jnp.broadcast_to(row, shape)
    zero = jnp.zeros(shape, row.dtype)
    return jnp.sum(jnp.where(rows_of(shape) == lanes_of(shape), spread, zero), axis=1, keepdims=True)


def as_row(column, size):
    shape = (size, size)
    spread = jnp.broadcast_to(column, shape)
    zero = jnp.zeros(shape, column.dtype)
    return jnp.sum(jnp.where(rows_of(shape) == lanes_of(shape), spread, zero), axis=0, keepdims=True)


def kernel(
    sizes,
    atm_hbm,
    ocean_hbm,
    atm_rate_hbm,
    ocean_rate_hbm,
    mask_hbm,
    weight_hbm,
    pair_src_hbm,
    pair_tgt_hbm,
    pair_count,
    atm_out,
    ocean_out,
    state,
    middle,
    result,
    weight,
    atm_rate,
    ocean_rate,
    mask,
    pair_src,
    pair_tgt,
    band,
    msg_out,
    msg_in,
    meta_out,
    meta_in,
    onehot,
    rate,
    rows_out,
    rows_in,
    cols_out,
    cols_in,
    table_v,
    table_s,
    load_sem,
    ring_send,
    ring_recv,
    sib_recv,
    halo_send,
    halo_recv,
    meta_send,
    meta_recv,
    msg_send,
    msg_recv,
    table_sem,
    out_sem,
):
    n_comp, n_tile, ch_a, ch_o, pairs = sizes
    n_z = n_tile // 2
    hops = n_z // 2
    groups = (ch_a + ch_o) // 8
    a_rows = ch_a * ROWS
    all_rows = (ch_a + ch_o) * ROWS
    s_rows = SURF * ROWS
    slots = n_tile * 8
    comp = lax.axis_index("comp")
    me = lax.axis_index("tile")
    z = me // 2
    core = me % 2
    sibling = z * 2 + 1 - core

    def load(i, src, dst):
        copy = pltpu.make_async_copy(src, dst, load_sem.at[i])
        copy.start()
        return copy

    surf_loads = (
        load(5, mask_hbm, mask),
        load(0, atm_hbm.at[pl.ds(0, s_rows)], state.at[pl.ds(0, s_rows)]),
        load(1, ocean_hbm.at[pl.ds(0, s_rows)], state.at[pl.ds(a_rows, s_rows)]),
    )
    rest_loads = [
        load(2, atm_hbm.at[pl.ds(s_rows, a_rows - s_rows)], state.at[pl.ds(s_rows, a_rows - s_rows)])
    ]
    if ch_o > SURF:
        rest_loads.append(
            load(
                3,
                ocean_hbm.at[pl.ds(s_rows, ch_o * ROWS - s_rows)],
                state.at[pl.ds(a_rows + s_rows, ch_o * ROWS - s_rows)],
            )
        )
    small_loads = [
        load(6, atm_rate_hbm, atm_rate),
        load(7, ocean_rate_hbm, ocean_rate),
        load(8, pair_src_hbm, pair_src),
        load(9, pair_tgt_hbm, pair_tgt),
    ]
    weight_load = load(4, weight_hbm, weight)

    barrier = pltpu.get_barrier_semaphore()
    north = lax.rem(comp + n_comp - 1, n_comp)
    south = lax.rem(comp + 1, n_comp)

    def greet(i, carry):
        pl.semaphore_signal(
            barrier, inc=1, device_id=(comp, lax.rem(me + i, n_tile)), device_id_type=MESH
        )
        return carry

    lax.fori_loop(1, n_tile, greet, 0)
    pl.semaphore_signal(barrier, inc=1, device_id=(north, me), device_id_type=MESH)
    pl.semaphore_signal(barrier, inc=1, device_id=(south, me), device_id_type=MESH)

    for copy in surf_loads:
        copy.wait()
    wet = jnp.broadcast_to(as_column(mask[...].astype(F32), ROWS), (ROWS, LANES))
    own = (core * n_z + z) * ROWS
    for y in range(ROWS):
        atm = state[pl.ds(y, 8, stride=ROWS), :]
        ocean = state[pl.ds(a_rows + y, 8, stride=ROWS), :] * wet[y : y + 1, :]
        band[own + y] = jnp.concatenate([atm, ocean], axis=0).astype(BF16)

    pl.semaphore_wait(barrier, n_tile + 1)

    half = ROWS // 2

    def block(owner_z, c):
        return band.at[pl.ds((core * n_z + owner_z) * ROWS + c * half, half)]

    def used(way, hop, c):
        return hop < hops - 1 or (hop == hops - 1 and c == way)

    def ring_copy(owner_z, way, hop, c):
        step = 1 if way == 0 else n_z - 1
        return pltpu.make_async_remote_copy(
            src_ref=block(owner_z, c),
            dst_ref=block(owner_z, c),
            send_sem=ring_send,
            recv_sem=ring_recv.at[way, hop, c],
            device_id=(comp, lax.rem(z + step, n_z) * 2 + core),
            device_id_type=MESH,
        )

    def sib_copy(owner_z, c):
        return pltpu.make_async_remote_copy(
            src_ref=block(owner_z, c),
            dst_ref=block(owner_z, c),
            send_sem=ring_send,
            recv_sem=sib_recv,
            device_id=(comp, sibling),
            device_id_type=MESH,
        )

    chunks = 0
    for c in range(2):
        for way in range(2):
            if used(way, 0, c):
                ring_copy(z, way, 0, c).start()
                chunks += 1
    for c in range(2):
        sib_copy(z, c).start()
        chunks += 1

    def service(hop):
        count = 0
        for c in range(2):
            for way in range(2):
                if not used(way, hop, c):
                    continue
                back = n_z - (hop + 1) if way == 0 else hop + 1
                owner_z = lax.rem(z + back, n_z)
                ring_copy(owner_z, way, hop, c).wait_recv()
                if used(way, hop + 1, c):
                    ring_copy(owner_z, way, hop + 1, c).start()
                    count += 1
                sib_copy(owner_z, c).start()
                count += 1
        return count

    lane8 = lanes_of((8, LANES))

    def pack(g, rows, turn):
        west = jnp.zeros((8, LANES), F32)
        east = jnp.zeros((8, LANES), F32)
        for y in range(ROWS):
            here = lane8 == y
            west = jnp.where(here, rows[y] if y == 0 else pltpu.roll(rows[y], y, 1), west)
            east = jnp.where(here, pltpu.roll(rows[y], y + 1, 1), east)
        shift = lax.rem(g, 8) * ROWS
        at = pl.ds(pl.multiple_of(g // 8 * 8, 8), 8)
        cols_out[turn, 0, at, :] = cols_out[turn, 0, at, :] + pltpu.roll(west, shift, 1)
        cols_out[turn, 1, at, :] = cols_out[turn, 1, at, :] + pltpu.roll(east, shift, 1)
        own8 = pl.ds(pl.multiple_of(g * 8, 8), 8)
        rows_out[turn, 0, own8, :] = rows[0]
        rows_out[turn, 1, own8, :] = rows[ROWS - 1]

    def group_rows(ref, g):
        return [ref[pl.ds(g * LANES + y, 8, stride=ROWS), :] for y in range(ROWS)]

    def halo_copies(turn):
        west_of, east_of = lax.rem(me + n_tile - 1, n_tile), lax.rem(me + 1, n_tile)
        plan = (
            (rows_out.at[turn, 0], rows_in.at[turn, 1], (north, me)),
            (rows_out.at[turn, 1], rows_in.at[turn, 0], (south, me)),
            (cols_out.at[turn, 0], cols_in.at[turn, 1], (comp, west_of)),
            (cols_out.at[turn, 1], cols_in.at[turn, 0], (comp, east_of)),
        )
        return [
            pltpu.make_async_remote_copy(
                src_ref=src,
                dst_ref=dst,
                send_sem=halo_send.at[turn, i],
                recv_sem=halo_recv.at[turn, i],
                device_id=to,
                device_id_type=MESH,
            )
            for i, (src, dst, to) in enumerate(plan)
        ]

    keep_north = (comp > 0).astype(F32)
    keep_south = (comp < n_comp - 1).astype(F32)

    def relax_group(g, source, target, turn):
        rows = group_rows(source, g)
        own8 = pl.ds(pl.multiple_of(g * 8, 8), 8)
        above = rows_in[turn, 0, own8, :] * keep_north
        below = rows_in[turn, 1, own8, :] * keep_south
        at = pl.ds(pl.multiple_of(g // 8 * 8, 8), 8)
        shift = lax.rem(LANES - lax.rem(g, 8) * ROWS, LANES)
        west = pltpu.roll(cols_in[turn, 0, at, :], shift, 1)
        east = pltpu.roll(cols_in[turn, 1, at, :], shift, 1)
        spread = rate[own8, :]
        new = []
        for y in range(ROWS):
            row = rows[y]
            left = pltpu.roll(
                jnp.where(lane8 == LANES - 1, pltpu.roll(west, LANES - 1 - y, 1), row), 1, 1
            )
            beyond = east if y == 0 else pltpu.roll(east, LANES - y, 1)
            right = pltpu.roll(jnp.where(lane8 == 0, beyond, row), LANES - 1, 1)
            up = above if y == 0 else rows[y - 1]
            down = below if y == ROWS - 1 else rows[y + 1]
            value = row + spread * (up + down + left + right - 4.0 * row)
            target[pl.ds(g * LANES + y, 8, stride=ROWS), :] = value
            new.append(value)
        return new

    cols_out[...] = jnp.zeros_like(cols_out)
    for copy in rest_loads:
        copy.wait()

    def first_pack(g, carry):
        pack(g, group_rows(state, g), 0)
        return carry

    lax.fori_loop(0, groups, first_pack, 0)
    halo_first = halo_copies(0)
    for copy in halo_first:
        copy.start()

    for copy in small_loads:
        copy.wait()
    rate[pl.ds(0, ch_a), :] = jnp.broadcast_to(as_column(atm_rate[...], ch_a), (ch_a, LANES))
    rate[pl.ds(ch_a, ch_o), :] = jnp.broadcast_to(as_column(ocean_rate[...], ch_o), (ch_o, LANES))

    pair_shape = (pairs, pairs)
    later = lanes_of(pair_shape) < rows_of(pair_shape)
    live_row = (lanes_of((1, pairs)) < pair_count[0, 0]).astype(jnp.int32)
    live_column = (rows_of((pairs, 1)) < pair_count[0, 0]).astype(jnp.int32)
    live_all = jnp.broadcast_to(live_row, pair_shape)
    pair_column = rows_of((pairs, 1))
    slot_lane = lanes_of((pairs, slots))
    slot_row = rows_of((slots, pairs))
    place, lines, y_of = [], [], []
    for codes in (pair_tgt, pair_src):
        code = codes[...]
        peer = code >> 4
        y_row = (code & 15).astype(F32)
        tile = ((peer & 1) * n_z + (peer >> 1)) * ROWS + (code & 15)
        peer_column = as_column(peer, pairs)
        before = jnp.logical_and(later, jnp.broadcast_to(peer, pair_shape) == peer_column)
        rank_column = jnp.sum(
            jnp.where(before, live_all, jnp.zeros_like(live_all)), axis=1, keepdims=True
        )
        rank_row = as_row(rank_column, pairs)
        slot_column = jnp.where(live_column > 0, peer_column * 8 + rank_column, -1)
        slot_of_row = jnp.where(live_row > 0, peer * 8 + rank_row, -1)
        place.append(as_column(tile, pairs))
        lines.append(slot_column == slot_lane)
        hot_rows = jnp.where(slot_row == slot_of_row, y_row - EMPTY, 0.0)
        y_of.append(jnp.sum(hot_rows, axis=1, keepdims=True) + EMPTY)
    table_v[...] = jnp.zeros_like(table_v)
    for i, (hot, values) in enumerate(
        ((lines[0], pair_column), (lines[0], place[1]), (lines[1], pair_column), (lines[1], place[0]))
    ):
        found = jnp.where(hot, jnp.broadcast_to(values, (pairs, slots)), jnp.zeros_like(slot_lane))
        table_v[i : i + 1, :] = jnp.sum(found, axis=0, keepdims=True)
    table_copy = pltpu.make_async_copy(table_v, table_s, table_sem)
    table_copy.start()
    meta_lane = lanes_of((slots, LANES))
    inside = (meta_lane >> 4) == lax.rem(me, 8)
    meta_out[...] = jnp.where(
        inside,
        jnp.where((meta_lane & 15) < 8, y_of[0], y_of[1]),
        0.0,
    )

    def meta_slot(e):
        return pl.ds(pl.multiple_of(e * 8, 8), 8)

    def send_meta(i, carry):
        e = lax.rem(me + i, n_tile)
        pltpu.make_async_remote_copy(
            src_ref=meta_out.at[meta_slot(e)],
            dst_ref=meta_in.at[meta_slot(me)],
            send_sem=meta_send,
            recv_sem=meta_recv,
            device_id=(comp, e),
            device_id_type=MESH,
        ).start()
        return carry

    lax.fori_loop(1, n_tile, send_meta, 0)
    pltpu.make_async_copy(
        meta_out.at[meta_slot(me)], meta_in.at[meta_slot(me)], meta_recv
    ).start()

    def first_step(g, carry):
        pack(g, relax_group(g, state, middle, 0), 1)
        return carry

    def second_step(g, carry):
        relax_group(g, middle, result, 1)
        return carry

    def build_onehot():
        pltpu.make_async_copy(meta_in, meta_in, meta_recv).wait()
        shape = (2 * s_rows, LANES)
        y_at = (rows_of(shape) & 15).astype(F32)
        field = rows_of(shape) >> 4
        same = field == (lanes_of(shape) & 15)
        per = min(8, n_tile)
        for part in range(n_tile // per):
            total = meta_in[pl.ds(part * per * 8, 8), :]
            for d in range(1, per):
                total = total + meta_in[pl.ds((part * per + d) * 8, 8), :]
            for r in range(CAP):
                hit = jnp.logical_and(same, total[r : r + 1, :] == y_at)
                start = r * n_tile * ROWS + part * LANES
                onehot[:, start : start + LANES] = jnp.where(hit, 1.0, 0.0).astype(BF16)

    done = []

    def halo_wait(copies):
        for copy in copies:
            copy.wait()

    cut = min(groups // 2, ch_a // 8)

    def work_a():
        halo_wait(halo_first)
        lax.fori_loop(0, cut, first_step, 0)

    def work_b():
        lax.fori_loop(cut, groups, first_step, 0)
        copies = halo_copies(1)
        for copy in copies:
            copy.start()
        done.append(copies)

    def work_c():
        halo_wait(done[0])
        lax.fori_loop(0, cut, second_step, 0)

    def work_d():
        lax.fori_loop(cut, groups, second_step, 0)

    stages = [work_a, work_b, build_onehot, work_c, work_d]
    for hop in range(hops):
        chunks += service(hop)
        if stages:
            stages.pop(0)()
    for stage in stages:
        stage()

    def write(i, src_row, dst, dst_row, size):
        copy = pltpu.make_async_copy(
            result.at[pl.ds(src_row, size)], dst.at[pl.ds(dst_row, size)], out_sem.at[i]
        )
        copy.start()
        return copy

    writes = [write(0, s_rows, atm_out, s_rows, a_rows - s_rows)]
    if ch_o > SURF:
        writes.append(write(1, a_rows + s_rows, ocean_out, s_rows, ch_o * ROWS - s_rows))

    weight_load.wait()
    table_copy.wait()
    theirs = band.at[pl.ds((1 - core) * n_z * ROWS, n_z * ROWS)]
    pltpu.make_async_copy(theirs, theirs, sib_recv).wait()

    top = rows_of((ROWS, LANES)) < 8

    def msg_slot(e):
        return pl.ds(pl.multiple_of(e * ROWS, ROWS), ROWS)

    def fill(e):
        for r in range(CAP):
            s = e * 8 + r
            ahead = jnp.dot(
                band[table_s[1, s]], weight[table_s[0, s]], preferred_element_type=F32
            )
            back = lax.dot_general(
                band[table_s[3, s]],
                weight[table_s[2, s]],
                (((1,), (1,)), ((), ())),
                preferred_element_type=F32,
            )
            msg_out[msg_slot(e), r * LANES : (r + 1) * LANES] = jnp.where(top, ahead, back).astype(
                BF16
            )

    def send(e):
        pltpu.make_async_remote_copy(
            src_ref=msg_out.at[msg_slot(e)],
            dst_ref=msg_in.at[msg_slot(me)],
            send_sem=msg_send,
            recv_sem=msg_recv,
            device_id=(comp, e),
            device_id_type=MESH,
        ).start()

    def far_to_near(i, carry):
        away = hops - (i + 1) // 2
        away = jnp.where(lax.rem(i, 2) == 1, away, n_z - away)
        other = lax.rem(z + away, n_z) * 2
        for k in range(2):
            fill(other + k)
            send(other + k)
        return carry

    lax.fori_loop(0, n_z - 1, far_to_near, 0)
    fill(sibling)
    send(sibling)
    fill(me)
    pltpu.make_async_copy(msg_out.at[msg_slot(me)], msg_in.at[msg_slot(me)], msg_recv).start()

    pltpu.make_async_copy(msg_in, msg_in, msg_recv).wait()
    force = jnp.zeros((2 * s_rows, LANES), F32)
    depth = n_tile * ROWS
    for r in range(CAP):
        force = force + jnp.dot(
            onehot[:, r * depth : (r + 1) * depth],
            msg_in[:, r * LANES : (r + 1) * LANES],
            preferred_element_type=F32,
        )
    wet_rows = jnp.concatenate([wet] * SURF, axis=0)
    result[pl.ds(0, s_rows), :] = result[pl.ds(0, s_rows), :] + force[s_rows:]
    writes.append(write(2, 0, atm_out, 0, s_rows))
    result[pl.ds(a_rows, s_rows), :] = result[pl.ds(a_rows, s_rows), :] + force[:s_rows] * wet_rows
    writes.append(write(3, a_rows, ocean_out, 0, s_rows))

    sent = band.at[pl.ds(0, chunks * half)]
    pltpu.make_async_copy(sent, sent, ring_send).wait()
    metas = meta_out.at[pl.ds(0, (n_tile - 1) * 8)]
    pltpu.make_async_copy(metas, metas, meta_send).wait()
    msgs = msg_out.at[pl.ds(0, (n_tile - 1) * ROWS)]
    pltpu.make_async_copy(msgs, msgs, msg_send).wait()
    for copy in writes:
        copy.wait()


def shards(
    n_comp,
    n_tile,
    atm_state,
    ocean_state,
    atm_rate,
    ocean_rate,
    ocean_mask,
    remap_weight,
    pair_src,
    pair_tgt,
    pair_count,
):
    ch_a, ch_o = atm_state.shape[0], ocean_state.shape[0]
    pairs = pair_src.shape[1]
    total = ch_a + ch_o
    a_rows, o_rows = ch_a * ROWS, ch_o * ROWS
    hops = n_tile // 4
    packed = (total // 8 + 7) // 8 * 8
    hbm = pl.BlockSpec(memory_space=pltpu.HBM)
    dma = pltpu.SemaphoreType.DMA
    atm_next, ocean_next = pl.pallas_call(
        functools.partial(kernel, (n_comp, n_tile, ch_a, ch_o, pairs)),
        out_shape=(
            jax.ShapeDtypeStruct((a_rows, LANES), F32),
            jax.ShapeDtypeStruct((o_rows, LANES), F32),
        ),
        in_specs=[hbm] * 8 + [pl.BlockSpec(memory_space=pltpu.SMEM)],
        out_specs=(hbm, hbm),
        scratch_shapes=[
            pltpu.VMEM((total * ROWS + ROWS, LANES), F32),
            pltpu.VMEM((total * ROWS + ROWS, LANES), F32),
            pltpu.VMEM((total * ROWS + ROWS, LANES), F32),
            pltpu.VMEM((pairs, LANES, LANES), BF16),
            pltpu.VMEM((1, ch_a), F32),
            pltpu.VMEM((1, ch_o), F32),
            pltpu.VMEM((1, ROWS), jnp.int32),
            pltpu.VMEM((1, pairs), jnp.int32),
            pltpu.VMEM((1, pairs), jnp.int32),
            pltpu.VMEM((n_tile * ROWS, 2 * SURF, LANES), BF16),
            pltpu.VMEM((n_tile * ROWS, CAP * LANES), BF16),
            pltpu.VMEM((n_tile * ROWS, CAP * LANES), BF16),
            pltpu.VMEM((n_tile * 8, LANES), F32),
            pltpu.VMEM((n_tile * 8, LANES), F32),
            pltpu.VMEM((2 * SURF * ROWS, CAP * n_tile * ROWS), BF16),
            pltpu.VMEM((total, LANES), F32),
            pltpu.VMEM((2, 2, total, LANES), F32),
            pltpu.VMEM((2, 2, total, LANES), F32),
            pltpu.VMEM((2, 2, packed, LANES), F32),
            pltpu.VMEM((2, 2, packed, LANES), F32),
            pltpu.VMEM((8, n_tile * 8), jnp.int32),
            pltpu.SMEM((8, n_tile * 8), jnp.int32),
            dma((10,)),
            dma,
            dma((2, hops, 2)),
            dma,
            dma((2, 4)),
            dma((2, 4)),
            dma,
            dma,
            dma,
            dma,
            dma,
            dma((4,)),
        ],
        compiler_params=pltpu.CompilerParams(
            collective_id=0, has_side_effects=True, vmem_limit_bytes=60 * 1024 * 1024
        ),
        name="coupled_interval",
    )(
        atm_state.reshape(a_rows, LANES),
        ocean_state.reshape(o_rows, LANES),
        atm_rate.reshape(1, ch_a),
        ocean_rate.reshape(1, ch_o),
        ocean_mask.reshape(1, ROWS),
        remap_weight.reshape(pairs, LANES, LANES),
        pair_src,
        pair_tgt,
        pair_count,
    )
    return atm_next.reshape(ch_a, ROWS, LANES), ocean_next.reshape(ch_o, ROWS, LANES)


def solution(mesh):
    return jax.shard_map(
        functools.partial(shards, mesh.shape["comp"], mesh.shape["tile"]),
        mesh=mesh,
        in_specs=(
            P(None, "comp", "tile"),
            P(None, "comp", "tile"),
            P(),
            P(),
            P("comp", "tile"),
            P("comp", "tile", None, None),
            P("comp", "tile"),
            P("comp", "tile"),
            P("comp", "tile"),
        ),
        out_specs=(P(None, "comp", "tile"), P(None, "comp", "tile")),
        check_vma=False,
    )
```

time: 193 us -> 67.3 us (0.35); the launches traced: 189 us -> 67.1 us
  Pallas kernels: 0 us -> 62.8 us
  blocking collectives: 59.5 us -> 0 us
  starting transfers between devices: 48 us -> 0 us
  local copies, waits for them, and re-layouts: 25.9 us -> 3.06 us
  waiting for transfers between devices: 17.2 us -> 0 us
  between operations: 15.1 us -> 1.3 us
  other arithmetic: 13.4 us -> 0 us
  matrix products: 10.4 us -> 0 us
    pallas_call x0 -> x1, Pallas kernels: none -> 62.8 us  [shards(): pl.pallas_call(functools.partial(kernel, (n_comp, n_tile, ch_a, ch_o, pai...]
    all_gather x2 -> x0, blocking collectives: 59.5 us -> none  [the longest x1 36.6 us: shards(): lax.all_gather(atm_source, 'tile', axis=1, tiled=True)]
    ppermute x16 -> x0, starting transfers between devices: 48 us -> none  [the longest x8 31.4 us: padded_2(): lax.ppermute(lax.slice_in_dim(block, 0, width, axis=dim), axis, backward)]
    reduce_scatter x1 -> x0, waiting for transfers between devices: 12.6 us -> none  [shards(): lax.psum_scatter(jnp.dot(ahead_hot, ahead_flat, precision=lax.Precision.H...]
    dot_general x4 -> x0, matrix products: 10.4 us -> none  [the longest x1 4.93 us: shards(): jnp.dot(back_hot, back_flat, precision=lax.Precision.HIGHEST, preferred_e...]
    scatter-add x1 -> x0, local copies, waits for them, and re-layouts: 5.74 us -> none  [shards(): atm_next = atm_stepped.at[:SURF].add(jnp.transpose(atm_force, (1, 0, 2)))]
    slice x11 -> x0, local copies, waits for them, and re-layouts: 5.32 us -> none  [the longest x7 3.41 us: padded_2(): lax.slice_in_dim(block, block.shape[dim] - width, None, axis=dim)]
    add x5 -> x0, other arithmetic: 4.75 us -> none  [the longest x4 2.42 us: relax(): return center + spread[:, None, None] * (beside_all - 4.0 * center)]
  transfers between devices with their start and end apart: 17 -> 0, of which waited for: 9 -> 0; matrix products, arithmetic and copies ran while one was open for 9% -> 0% of each run, Pallas kernels for 0% -> 0%
where the time goes in v1:
time: 67.3 us; the launch traced here: 67.1 us
  Pallas kernels  62.8 us (93%)
  local copies, waits for them, and re-layouts  3.06 us (5%)
  between operations  1.3 us (2%)
    pallas_call x1, Pallas kernels, shards(): pl.pallas_call(functools.partial(kernel, (n_comp, n_tile, ch_a, ch_o, pai...  62.8 us
    unnamed x4, local copies, waits for them, and re-layouts  3.06 us

profile of v1, /device:TPU:1, one launch (start us, length us, event | category | flops | bytes accessed | tf_op | source)
XLA Modules:
  0.0 67.1 jit_solution(16525867245110861874)
XLA Ops:
  1.3 62.8 %coupled_interval.1 = (f32[2048,128]{1,0:T(8,128)}, f32[768,128]{1,0:T(8,128)}) custom-call(f32[2048,128]{1,0:T(8,128)} %bitcast.9, f32[768,128]{1,0:T(8,128)} %bitcast.11, f32[1,128]{1,0:T(1,128)} %bitcast.13, f32[1,48]{1,0:T(1,128)} %bitcast.14, s32[1,16]{1,0:T(1,128)} %bitcast.15, bf16[48,128,128]{2,1,0:T(8,128)(2,1)} %bitcast.8, s32[1,48]{1,0:T(1,128)} %pair_src_hbm.1, ...), custom_call_target="tpu_custom_call" | custom-call | tf_op jit(solution)/shard_map/coupled_interval/pallas_call | solution.py:527
  64.1 0.0 copy-start
  64.1 2.3 %copy.14 = f32[128,16,128]{2,1,0:T(8,128)} copy(f32[128,16,128]{2,1,0:T(8,128)} %bitcast.10) | data formatting | bytes 2097152
  66.4 0.0 copy-done
  66.4 0.7 %copy.15 = f32[48,16,128]{2,1,0:T(8,128)} copy(f32[48,16,128]{2,1,0:T(8,128)S(1)} %bitcast.12) | data formatting | bytes 786432
Async XLA Ops:
  64.1 2.3 %copy-start = (f32[768,128]{1,0:T(8,128)S(1)}, f32[768,128]{1,0:T(8,128)}, u32[]{:S(2)}) copy-start(f32[768,128]{1,0:T(8,128)} %get-tuple-element.5) | copy-start | bytes 1179652

commit v2 on v1

--- a/solution.py
+++ b/solution.py
@@ -11,7 +11,7 @@
 LANES = 128
 ROWS = 16
 CAP = 3
-EMPTY = 100.0
+EMPTY = 16
 F32 = jnp.float32
 BF16 = jnp.bfloat16
 MESH = pl.DeviceIdType.MESH
@@ -61,7 +61,9 @@
     mask,
     pair_src,
     pair_tgt,
-    band,
+    own,
+    tile_out,
+    tile_in,
     msg_out,
     msg_in,
     meta_out,
@@ -74,10 +76,11 @@
     cols_in,
     table_v,
     table_s,
+    asked_v,
+    asked_s,
     load_sem,
-    ring_send,
-    ring_recv,
-    sib_recv,
+    tile_send,
+    tile_recv,
     halo_send,
     halo_recv,
     meta_send,
@@ -85,6 +88,7 @@
     msg_send,
     msg_recv,
     table_sem,
+    asked_sem,
     out_sem,
 ):
     n_comp, n_tile, ch_a, ch_o, pairs = sizes
@@ -144,71 +148,83 @@
     pl.semaphore_signal(barrier, inc=1, device_id=(north, me), device_id_type=MESH)
     pl.semaphore_signal(barrier, inc=1, device_id=(south, me), device_id_type=MESH)
 
+    for copy in small_loads:
+        copy.wait()
+
+    pair_shape = (pairs, pairs)
+    later = lanes_of(pair_shape) < rows_of(pair_shape)
+    live_row = (lanes_of((1, pairs)) < pair_count[0, 0]).astype(jnp.int32)
+    live_column = (rows_of((pairs, 1)) < pair_count[0, 0]).astype(jnp.int32)
+    live_all = jnp.broadcast_to(live_row, pair_shape)
+    pair_column = rows_of((pairs, 1))
+    slot_lane = lanes_of((pairs, slots))
+    slot_row = rows_of((slots, pairs))
+    place, lines, y_of = [], [], []
+    for codes in (pair_tgt, pair_src):
+        code = codes[...]
+        peer = code >> 4
+        y_row = code & 15
+        peer_column = as_column(peer, pairs)
+        before = jnp.logical_and(later, jnp.broadcast_to(peer, pair_shape) == peer_column)
+        rank_column = jnp.sum(
+            jnp.where(before, live_all, jnp.zeros_like(live_all)), axis=1, keepdims=True
+        )
+        rank_row = as_row(rank_column, pairs)
+        slot_column = jnp.where(live_column > 0, peer_column * 8 + rank_column, -1)
+        slot_of_row = jnp.where(live_row > 0, peer * 8 + rank_row, -1)
+        place.append(peer_column * CAP + rank_column)
+        lines.append(slot_column == slot_lane)
+        hot_rows = jnp.where(slot_row == slot_of_row, jnp.broadcast_to(y_row - EMPTY, (slots, pairs)), jnp.zeros_like(slot_row))
+        y_of.append(jnp.sum(hot_rows, axis=1, keepdims=True) + EMPTY)
+    table_v[...] = jnp.zeros_like(table_v)
+    for i, (hot, values) in enumerate(
+        ((lines[0], pair_column), (lines[0], place[1]), (lines[1], pair_column), (lines[1], place[0]))
+    ):
+        found = jnp.where(hot, jnp.broadcast_to(values, (pairs, slots)), jnp.zeros_like(slot_lane))
+        table_v[i : i + 1, :] = jnp.sum(found, axis=0, keepdims=True)
+    table_copy = pltpu.make_async_copy(table_v, table_s, table_sem)
+    table_copy.start()
+    meta_lane = lanes_of((slots, LANES))
+    inside = (meta_lane >> 4) == lax.rem(me, 8)
+    meta_out[...] = jnp.where(
+        inside,
+        jnp.where(
+            (meta_lane & 15) < 8,
+            jnp.broadcast_to(y_of[0], (slots, LANES)),
+            jnp.broadcast_to(y_of[1], (slots, LANES)),
+        ),
+        jnp.zeros_like(meta_lane),
+    )
+
+    def meta_slot(e):
+        return pl.ds(pl.multiple_of(e * 8, 8), 8)
+
+    def send_meta(i, carry):
+        e = lax.rem(me + i, n_tile)
+        pltpu.make_async_remote_copy(
+            src_ref=meta_out.at[meta_slot(e)],
+            dst_ref=meta_in.at[meta_slot(me)],
+            send_sem=meta_send,
+            recv_sem=meta_recv,
+            device_id=(comp, e),
+            device_id_type=MESH,
+        ).start()
+        return carry
+
+    pl.semaphore_wait(barrier, n_tile + 1)
+    lax.fori_loop(1, n_tile, send_meta, 0)
+    pltpu.make_async_copy(
+        meta_out.at[meta_slot(me)], meta_in.at[meta_slot(me)], meta_recv
+    ).start()
+
     for copy in surf_loads:
         copy.wait()
     wet = jnp.broadcast_to(as_column(mask[...].astype(F32), ROWS), (ROWS, LANES))
-    own = (core * n_z + z) * ROWS
     for y in range(ROWS):
-        atm = state[pl.ds(y, 8, stride=ROWS), :]
-        ocean = state[pl.ds(a_rows + y, 8, stride=ROWS), :] * wet[y : y + 1, :]
-        band[own + y] = jnp.concatenate([atm, ocean], axis=0).astype(BF16)
-
-    pl.semaphore_wait(barrier, n_tile + 1)
-
-    half = ROWS // 2
-
-    def block(owner_z, c):
-        return band.at[pl.ds((core * n_z + owner_z) * ROWS + c * half, half)]
-
-    def used(way, hop, c):
-        return hop < hops - 1 or (hop == hops - 1 and c == way)
-
-    def ring_copy(owner_z, way, hop, c):
-        step = 1 if way == 0 else n_z - 1
-        return pltpu.make_async_remote_copy(
-            src_ref=block(owner_z, c),
-            dst_ref=block(owner_z, c),
-            send_sem=ring_send,
-            recv_sem=ring_recv.at[way, hop, c],
-            device_id=(comp, lax.rem(z + step, n_z) * 2 + core),
-            device_id_type=MESH,
-        )
-
-    def sib_copy(owner_z, c):
-        return pltpu.make_async_remote_copy(
-            src_ref=block(owner_z, c),
-            dst_ref=block(owner_z, c),
-            send_sem=ring_send,
-            recv_sem=sib_recv,
-            device_id=(comp, sibling),
-            device_id_type=MESH,
-        )
-
-    chunks = 0
-    for c in range(2):
-        for way in range(2):
-            if used(way, 0, c):
-                ring_copy(z, way, 0, c).start()
-                chunks += 1
-    for c in range(2):
-        sib_copy(z, c).start()
-        chunks += 1
-
-    def service(hop):
-        count = 0
-        for c in range(2):
-            for way in range(2):
-                if not used(way, hop, c):
-                    continue
-                back = n_z - (hop + 1) if way == 0 else hop + 1
-                owner_z = lax.rem(z + back, n_z)
-                ring_copy(owner_z, way, hop, c).wait_recv()
-                if used(way, hop + 1, c):
-                    ring_copy(owner_z, way, hop + 1, c).start()
-                    count += 1
-                sib_copy(owner_z, c).start()
-                count += 1
-        return count
+        air = state[pl.ds(y, 8, stride=ROWS), :]
+        sea = state[pl.ds(a_rows + y, 8, stride=ROWS), :] * wet[y : y + 1, :]
+        own[y] = jnp.concatenate([air, sea], axis=0).astype(BF16)
+
 
     lane8 = lanes_of((8, LANES))
 
@@ -291,72 +307,64 @@
     for copy in halo_first:
         copy.start()
 
-    for copy in small_loads:
-        copy.wait()
     rate[pl.ds(0, ch_a), :] = jnp.broadcast_to(as_column(atm_rate[...], ch_a), (ch_a, LANES))
     rate[pl.ds(ch_a, ch_o), :] = jnp.broadcast_to(as_column(ocean_rate[...], ch_o), (ch_o, LANES))
 
-    pair_shape = (pairs, pairs)
-    later = lanes_of(pair_shape) < rows_of(pair_shape)
-    live_row = (lanes_of((1, pairs)) < pair_count[0, 0]).astype(jnp.int32)
-    live_column = (rows_of((pairs, 1)) < pair_count[0, 0]).astype(jnp.int32)
-    live_all = jnp.broadcast_to(live_row, pair_shape)
-    pair_column = rows_of((pairs, 1))
-    slot_lane = lanes_of((pairs, slots))
-    slot_row = rows_of((slots, pairs))
-    place, lines, y_of = [], [], []
-    for codes in (pair_tgt, pair_src):
-        code = codes[...]
-        peer = code >> 4
-        y_row = (code & 15).astype(F32)
-        tile = ((peer & 1) * n_z + (peer >> 1)) * ROWS + (code & 15)
-        peer_column = as_column(peer, pairs)
-        before = jnp.logical_and(later, jnp.broadcast_to(peer, pair_shape) == peer_column)
-        rank_column = jnp.sum(
-            jnp.where(before, live_all, jnp.zeros_like(live_all)), axis=1, keepdims=True
-        )
-        rank_row = as_row(rank_column, pairs)
-        slot_column = jnp.where(live_column > 0, peer_column * 8 + rank_column, -1)
-        slot_of_row = jnp.where(live_row > 0, peer * 8 + rank_row, -1)
-        place.append(as_column(tile, pairs))
-        lines.append(slot_column == slot_lane)
-        hot_rows = jnp.where(slot_row == slot_of_row, y_row - EMPTY, 0.0)
-        y_of.append(jnp.sum(hot_rows, axis=1, keepdims=True) + EMPTY)
-    table_v[...] = jnp.zeros_like(table_v)
-    for i, (hot, values) in enumerate(
-        ((lines[0], pair_column), (lines[0], place[1]), (lines[1], pair_column), (lines[1], place[0]))
-    ):
-        found = jnp.where(hot, jnp.broadcast_to(values, (pairs, slots)), jnp.zeros_like(slot_lane))
-        table_v[i : i + 1, :] = jnp.sum(found, axis=0, keepdims=True)
-    table_copy = pltpu.make_async_copy(table_v, table_s, table_sem)
-    table_copy.start()
-    meta_lane = lanes_of((slots, LANES))
-    inside = (meta_lane >> 4) == lax.rem(me, 8)
-    meta_out[...] = jnp.where(
-        inside,
-        jnp.where((meta_lane & 15) < 8, y_of[0], y_of[1]),
-        0.0,
-    )
-
-    def meta_slot(e):
-        return pl.ds(pl.multiple_of(e * 8, 8), 8)
-
-    def send_meta(i, carry):
-        e = lax.rem(me + i, n_tile)
+    per = min(8, n_tile)
+    parts = n_tile // per
+    pltpu.make_async_copy(meta_in, meta_in, meta_recv).wait()
+    for part in range(parts):
+        total = meta_in[pl.ds(part * per * 8, 8), :]
+        for d in range(1, per):
+            total = total + meta_in[pl.ds((part * per + d) * 8, 8), :]
+        asked_v[pl.ds(part * 8, 8), :] = total
+    asked_copy = pltpu.make_async_copy(asked_v, asked_s, asked_sem)
+    asked_copy.start()
+
+    def build_onehot():
+        shape = (2 * s_rows, LANES)
+        y_at = rows_of(shape) & 15
+        same = (rows_of(shape) >> 4) == (lanes_of(shape) & 15)
+        for part in range(parts):
+            total = asked_v[pl.ds(part * 8, 8), :]
+            for r in range(CAP):
+                hit = jnp.logical_and(same, jnp.broadcast_to(total[r : r + 1, :], shape) == y_at)
+                start = r * n_tile * ROWS + part * LANES
+                onehot[:, start : start + LANES] = jnp.where(hit, 1.0, 0.0).astype(BF16)
+
+    top = rows_of((ROWS, LANES)) < 8
+
+    def over_peers(fill, send):
+        def far_to_near(i, carry):
+            away = hops - (i + 1) // 2
+            away = jnp.where(lax.rem(i, 2) == 1, away, n_z - away)
+            other = lax.rem(z + away, n_z) * 2
+            for k in range(2):
+                fill(other + k)
+                send(other + k)
+            return carry
+
+        lax.fori_loop(0, n_z - 1, far_to_near, 0)
+        fill(sibling)
+        send(sibling)
+        fill(me)
+
+    def pick(d):
+        for r in range(CAP):
+            row, lane = d // per * 8 + r, lax.rem(d, per) * ROWS
+            sea = asked_s[row, lane] & 15
+            air = asked_s[row, lane + 8] & 15
+            tile_out[d * CAP + r] = jnp.where(top, own[air], own[sea])
+
+    def send_tiles(d):
         pltpu.make_async_remote_copy(
-            src_ref=meta_out.at[meta_slot(e)],
-            dst_ref=meta_in.at[meta_slot(me)],
-            send_sem=meta_send,
-            recv_sem=meta_recv,
-            device_id=(comp, e),
+            src_ref=tile_out.at[pl.ds(d * CAP, CAP)],
+            dst_ref=tile_in.at[pl.ds(me * CAP, CAP)],
+            send_sem=tile_send,
+            recv_sem=tile_recv,
+            device_id=(comp, d),
             device_id_type=MESH,
         ).start()
-        return carry
-
-    lax.fori_loop(1, n_tile, send_meta, 0)
-    pltpu.make_async_copy(
-        meta_out.at[meta_slot(me)], meta_in.at[meta_slot(me)], meta_recv
-    ).start()
 
     def first_step(g, carry):
         pack(g, relax_group(g, state, middle, 0), 1)
@@ -366,56 +374,19 @@
         relax_group(g, middle, result, 1)
         return carry
 
-    def build_onehot():
-        pltpu.make_async_copy(meta_in, meta_in, meta_recv).wait()
-        shape = (2 * s_rows, LANES)
-        y_at = (rows_of(shape) & 15).astype(F32)
-        field = rows_of(shape) >> 4
-        same = field == (lanes_of(shape) & 15)
-        per = min(8, n_tile)
-        for part in range(n_tile // per):
-            total = meta_in[pl.ds(part * per * 8, 8), :]
-            for d in range(1, per):
-                total = total + meta_in[pl.ds((part * per + d) * 8, 8), :]
-            for r in range(CAP):
-                hit = jnp.logical_and(same, total[r : r + 1, :] == y_at)
-                start = r * n_tile * ROWS + part * LANES
-                onehot[:, start : start + LANES] = jnp.where(hit, 1.0, 0.0).astype(BF16)
-
-    done = []
-
-    def halo_wait(copies):
-        for copy in copies:
-            copy.wait()
-
-    cut = min(groups // 2, ch_a // 8)
-
-    def work_a():
-        halo_wait(halo_first)
-        lax.fori_loop(0, cut, first_step, 0)
-
-    def work_b():
-        lax.fori_loop(cut, groups, first_step, 0)
-        copies = halo_copies(1)
-        for copy in copies:
-            copy.start()
-        done.append(copies)
-
-    def work_c():
-        halo_wait(done[0])
-        lax.fori_loop(0, cut, second_step, 0)
-
-    def work_d():
-        lax.fori_loop(cut, groups, second_step, 0)
-
-    stages = [work_a, work_b, build_onehot, work_c, work_d]
-    for hop in range(hops):
-        chunks += service(hop)
-        if stages:
-            stages.pop(0)()
-    for stage in stages:
-        stage()
-
+    asked_copy.wait()
+    over_peers(pick, send_tiles)
+    pltpu.make_async_copy(
+        tile_out.at[pl.ds(me * CAP, CAP)], tile_in.at[pl.ds(me * CAP, CAP)], tile_recv
+    ).start()
+
+    build_onehot()
+    for copy in halo_first:
+        copy.wait()
+    lax.fori_loop(0, groups, first_step, 0, unroll=2)
+    halo_second = halo_copies(1)
+    for copy in halo_second:
+        copy.start()
     def write(i, src_row, dst, dst_row, size):
         copy = pltpu.make_async_copy(
             result.at[pl.ds(src_row, size)], dst.at[pl.ds(dst_row, size)], out_sem.at[i]
@@ -423,16 +394,9 @@
         copy.start()
         return copy
 
-    writes = [write(0, s_rows, atm_out, s_rows, a_rows - s_rows)]
-    if ch_o > SURF:
-        writes.append(write(1, a_rows + s_rows, ocean_out, s_rows, ch_o * ROWS - s_rows))
-
     weight_load.wait()
     table_copy.wait()
-    theirs = band.at[pl.ds((1 - core) * n_z * ROWS, n_z * ROWS)]
-    pltpu.make_async_copy(theirs, theirs, sib_recv).wait()
-
-    top = rows_of((ROWS, LANES)) < 8
+    pltpu.make_async_copy(tile_in, tile_in, tile_recv).wait()
 
     def msg_slot(e):
         return pl.ds(pl.multiple_of(e * ROWS, ROWS), ROWS)
@@ -441,10 +405,10 @@
         for r in range(CAP):
             s = e * 8 + r
             ahead = jnp.dot(
-                band[table_s[1, s]], weight[table_s[0, s]], preferred_element_type=F32
+                tile_in[table_s[1, s]], weight[table_s[0, s]], preferred_element_type=F32
             )
             back = lax.dot_general(
-                band[table_s[3, s]],
+                tile_in[table_s[3, s]],
                 weight[table_s[2, s]],
                 (((1,), (1,)), ((), ())),
                 preferred_element_type=F32,
@@ -463,20 +427,16 @@
             device_id_type=MESH,
         ).start()
 
-    def far_to_near(i, carry):
-        away = hops - (i + 1) // 2
-        away = jnp.where(lax.rem(i, 2) == 1, away, n_z - away)
-        other = lax.rem(z + away, n_z) * 2
-        for k in range(2):
-            fill(other + k)
-            send(other + k)
-        return carry
-
-    lax.fori_loop(0, n_z - 1, far_to_near, 0)
-    fill(sibling)
-    send(sibling)
-    fill(me)
+    over_peers(fill, send)
     pltpu.make_async_copy(msg_out.at[msg_slot(me)], msg_in.at[msg_slot(me)], msg_recv).start()
+
+    for copy in halo_second:
+        copy.wait()
+    lax.fori_loop(0, groups, second_step, 0, unroll=2)
+
+    writes = [write(0, s_rows, atm_out, s_rows, a_rows - s_rows)]
+    if ch_o > SURF:
+        writes.append(write(1, a_rows + s_rows, ocean_out, s_rows, ch_o * ROWS - s_rows))
 
     pltpu.make_async_copy(msg_in, msg_in, msg_recv).wait()
     force = jnp.zeros((2 * s_rows, LANES), F32)
@@ -493,13 +453,33 @@
     result[pl.ds(a_rows, s_rows), :] = result[pl.ds(a_rows, s_rows), :] + force[:s_rows] * wet_rows
     writes.append(write(3, a_rows, ocean_out, 0, s_rows))
 
-    sent = band.at[pl.ds(0, chunks * half)]
-    pltpu.make_async_copy(sent, sent, ring_send).wait()
+    tiles = tile_out.at[pl.ds(0, (n_tile - 1) * CAP)]
+    pltpu.make_async_copy(tiles, tiles, tile_send).wait()
     metas = meta_out.at[pl.ds(0, (n_tile - 1) * 8)]
     pltpu.make_async_copy(metas, metas, meta_send).wait()
     msgs = msg_out.at[pl.ds(0, (n_tile - 1) * ROWS)]
     pltpu.make_async_copy(msgs, msgs, msg_send).wait()
     for copy in writes:
+        copy.wait()
+
+
+def hand_over(atm, ocean, atm_out, ocean_out, atm_held, ocean_held, in_sem, out_sem):
+    arrivals, departures = [], []
+    for source, held, target, parts in (
+        (atm, atm_held, atm_out, 8),
+        (ocean, ocean_held, ocean_out, 3),
+    ):
+        size = source.shape[0] // parts
+        for part in range(parts):
+            rows, i = pl.ds(part * size, size), len(arrivals)
+            arrivals.append(pltpu.make_async_copy(source.at[rows], held.at[rows], in_sem.at[i]))
+            departures.append(pltpu.make_async_copy(held.at[rows], target.at[rows], out_sem.at[i]))
+    for copy in arrivals:
+        copy.start()
+    for arrival, departure in zip(arrivals, departures):
+        arrival.wait()
+        departure.start()
+    for copy in departures:
         copy.wait()
 
 
@@ -520,7 +500,6 @@
     pairs = pair_src.shape[1]
     total = ch_a + ch_o
     a_rows, o_rows = ch_a * ROWS, ch_o * ROWS
-    hops = n_tile // 4
     packed = (total // 8 + 7) // 8 * 8
     hbm = pl.BlockSpec(memory_space=pltpu.HBM)
     dma = pltpu.SemaphoreType.DMA
@@ -542,11 +521,13 @@
             pltpu.VMEM((1, ROWS), jnp.int32),
             pltpu.VMEM((1, pairs), jnp.int32),
             pltpu.VMEM((1, pairs), jnp.int32),
-            pltpu.VMEM((n_tile * ROWS, 2 * SURF, LANES), BF16),
+            pltpu.VMEM((ROWS, 2 * SURF, LANES), BF16),
+            pltpu.VMEM((n_tile * CAP, 2 * SURF, LANES), BF16),
+            pltpu.VMEM((n_tile * CAP, 2 * SURF, LANES), BF16),
             pltpu.VMEM((n_tile * ROWS, CAP * LANES), BF16),
             pltpu.VMEM((n_tile * ROWS, CAP * LANES), BF16),
-            pltpu.VMEM((n_tile * 8, LANES), F32),
-            pltpu.VMEM((n_tile * 8, LANES), F32),
+            pltpu.VMEM((n_tile * 8, LANES), jnp.int32),
+            pltpu.VMEM((n_tile * 8, LANES), jnp.int32),
             pltpu.VMEM((2 * SURF * ROWS, CAP * n_tile * ROWS), BF16),
             pltpu.VMEM((total, LANES), F32),
             pltpu.VMEM((2, 2, total, LANES), F32),
@@ -555,12 +536,14 @@
             pltpu.VMEM((2, 2, packed, LANES), F32),
             pltpu.VMEM((8, n_tile * 8), jnp.int32),
             pltpu.SMEM((8, n_tile * 8), jnp.int32),
+            pltpu.VMEM(((n_tile + 7) // 8 * 8, LANES), jnp.int32),
+            pltpu.SMEM(((n_tile + 7) // 8 * 8, LANES), jnp.int32),
             dma((10,)),
             dma,
-            dma((2, hops, 2)),
             dma,
             dma((2, 4)),
             dma((2, 4)),
+            dma,
             dma,
             dma,
             dma,
@@ -583,6 +566,23 @@
         pair_tgt,
         pair_count,
     )
+    atm_next, ocean_next = pl.pallas_call(
+        hand_over,
+        out_shape=(
+            jax.ShapeDtypeStruct((a_rows, LANES), F32),
+            jax.ShapeDtypeStruct((o_rows, LANES), F32),
+        ),
+        in_specs=[hbm, hbm],
+        out_specs=(hbm, hbm),
+        scratch_shapes=[
+            pltpu.VMEM((a_rows, LANES), F32),
+            pltpu.VMEM((o_rows, LANES), F32),
+            dma((11,)),
+            dma((11,)),
+        ],
+        compiler_params=pltpu.CompilerParams(vmem_limit_bytes=60 * 1024 * 1024),
+        name="hand_over",
+    )(atm_next, ocean_next)
     return atm_next.reshape(ch_a, ROWS, LANES), ocean_next.reshape(ch_o, ROWS, LANES)
 
 

time: 67.3 us -> 54.9 us (0.82)
  Pallas kernels: 62.8 us -> 53.4 us
  local copies, waits for them, and re-layouts: 3.06 us -> 0 us
    pallas_call x1, Pallas kernels: 62.8 us -> 51.1 us  [shards(): pl.pallas_call(functools.partial(kernel, (n_comp, n_tile, ch_a, ch_o, pai...]
    unnamed x4 -> x0, local copies, waits for them, and re-layouts: 3.06 us -> none
    pallas_call x0 -> x1, Pallas kernels: none -> 2.27 us  [shards(): pl.pallas_call(hand_over, out_shape=(jax.ShapeDtypeStruct((a_rows, LANES)...]
where the time goes in v2:
time: 54.9 us; the launch traced here: 54.7 us
  Pallas kernels  53.4 us (97%)
  between operations  1.29 us (2%)
    pallas_call x1, Pallas kernels, shards(): pl.pallas_call(functools.partial(kernel, (n_comp, n_tile, ch_a, ch_o, pai...  51.1 us
    pallas_call x1, Pallas kernels, shards(): pl.pallas_call(hand_over, out_shape=(jax.ShapeDtypeStruct((a_rows, LANES)...  2.27 us

profile of v2, /device:TPU:1, one launch (start us, length us, event | category | flops | bytes accessed | tf_op | source)
XLA Modules:
  0.0 54.7 jit_solution(9289450326496305953)
XLA Ops:
  1.3 51.1 %coupled_interval.1 = (f32[2048,128]{1,0:T(8,128)}, f32[768,128]{1,0:T(8,128)}) custom-call(f32[2048,128]{1,0:T(8,128)} %bitcast.9, f32[768,128]{1,0:T(8,128)} %bitcast.10, f32[1,128]{1,0:T(1,128)} %bitcast.11, f32[1,48]{1,0:T(1,128)} %bitcast.12, s32[1,16]{1,0:T(1,128)} %bitcast.13, bf16[48,128,128]{2,1,0:T(8,128)(2,1)} %bitcast.8, s32[1,48]{1,0:T(1,128)} %pair_src_hbm.1, ...), custom_call_target="tpu_custom_call" | custom-call | tf_op jit(solution)/shard_map/coupled_interval/pallas_call | solution.py:506
  52.4 2.3 %hand_over.1 = (f32[2048,128]{1,0:T(8,128)}, f32[768,128]{1,0:T(8,128)}) custom-call(f32[2048,128]{1,0:T(8,128)} %get-tuple-element.6.atm, f32[768,128]{1,0:T(8,128)} %get-tuple-element.7.ocean), custom_call_target="tpu_custom_call" | custom-call | tf_op jit(solution)/shard_map/hand_over/pallas_call | solution.py:569

commit v3 on v2

--- a/solution.py
+++ b/solution.py
@@ -176,14 +176,6 @@
         lines.append(slot_column == slot_lane)
         hot_rows = jnp.where(slot_row == slot_of_row, jnp.broadcast_to(y_row - EMPTY, (slots, pairs)), jnp.zeros_like(slot_row))
         y_of.append(jnp.sum(hot_rows, axis=1, keepdims=True) + EMPTY)
-    table_v[...] = jnp.zeros_like(table_v)
-    for i, (hot, values) in enumerate(
-        ((lines[0], pair_column), (lines[0], place[1]), (lines[1], pair_column), (lines[1], place[0]))
-    ):
-        found = jnp.where(hot, jnp.broadcast_to(values, (pairs, slots)), jnp.zeros_like(slot_lane))
-        table_v[i : i + 1, :] = jnp.sum(found, axis=0, keepdims=True)
-    table_copy = pltpu.make_async_copy(table_v, table_s, table_sem)
-    table_copy.start()
     meta_lane = lanes_of((slots, LANES))
     inside = (meta_lane >> 4) == lax.rem(me, 8)
     meta_out[...] = jnp.where(
@@ -307,9 +299,6 @@
     for copy in halo_first:
         copy.start()
 
-    rate[pl.ds(0, ch_a), :] = jnp.broadcast_to(as_column(atm_rate[...], ch_a), (ch_a, LANES))
-    rate[pl.ds(ch_a, ch_o), :] = jnp.broadcast_to(as_column(ocean_rate[...], ch_o), (ch_o, LANES))
-
     per = min(8, n_tile)
     parts = n_tile // per
     pltpu.make_async_copy(meta_in, meta_in, meta_recv).wait()
@@ -379,6 +368,17 @@
     pltpu.make_async_copy(
         tile_out.at[pl.ds(me * CAP, CAP)], tile_in.at[pl.ds(me * CAP, CAP)], tile_recv
     ).start()
+
+    table_v[...] = jnp.zeros_like(table_v)
+    for i, (hot, values) in enumerate(
+        ((lines[0], pair_column), (lines[0], place[1]), (lines[1], pair_column), (lines[1], place[0]))
+    ):
+        found = jnp.where(hot, jnp.broadcast_to(values, (pairs, slots)), jnp.zeros_like(slot_lane))
+        table_v[i : i + 1, :] = jnp.sum(found, axis=0, keepdims=True)
+    table_copy = pltpu.make_async_copy(table_v, table_s, table_sem)
+    table_copy.start()
+    rate[pl.ds(0, ch_a), :] = jnp.broadcast_to(as_column(atm_rate[...], ch_a), (ch_a, LANES))
+    rate[pl.ds(ch_a, ch_o), :] = jnp.broadcast_to(as_column(ocean_rate[...], ch_o), (ch_o, LANES))
 
     build_onehot()
     for copy in halo_first:

time: 54.9 us -> 54.9 us (level)
  no operation moved by 1% of the time
where the time goes in v3:
time: 54.9 us; the launch traced here: 54.7 us
  Pallas kernels  53.4 us (97%)
  between operations  1.29 us (2%)
    pallas_call x1, Pallas kernels, shards(): pl.pallas_call(functools.partial(kernel, (n_comp, n_tile, ch_a, ch_o, pai...  51.2 us
    pallas_call x1, Pallas kernels, shards(): pl.pallas_call(hand_over, out_shape=(jax.ShapeDtypeStruct((a_rows, LANES)...  2.27 us

profile of v3, /device:TPU:1, one launch (start us, length us, event | category | flops | bytes accessed | tf_op | source)
XLA Modules:
  0.0 54.7 jit_solution(4764358892278851357)
XLA Ops:
  1.3 51.2 %coupled_interval.1 = (f32[2048,128]{1,0:T(8,128)}, f32[768,128]{1,0:T(8,128)}) custom-call(f32[2048,128]{1,0:T(8,128)} %bitcast.9, f32[768,128]{1,0:T(8,128)} %bitcast.10, f32[1,128]{1,0:T(1,128)} %bitcast.11, f32[1,48]{1,0:T(1,128)} %bitcast.12, s32[1,16]{1,0:T(1,128)} %bitcast.13, bf16[48,128,128]{2,1,0:T(8,128)(2,1)} %bitcast.8, s32[1,48]{1,0:T(1,128)} %pair_src_hbm.1, ...), custom_call_target="tpu_custom_call" | custom-call | tf_op jit(solution)/shard_map/coupled_interval/pallas_call | solution.py:506
  52.4 2.3 %hand_over.1 = (f32[2048,128]{1,0:T(8,128)}, f32[768,128]{1,0:T(8,128)}) custom-call(f32[2048,128]{1,0:T(8,128)} %get-tuple-element.6.atm, f32[768,128]{1,0:T(8,128)} %get-tuple-element.7.ocean), custom_call_target="tpu_custom_call" | custom-call | tf_op jit(solution)/shard_map/hand_over/pallas_call | solution.py:569
